TPU v7x, 128 devices: a whole 4x4x4 slice. The times are simulated.
128 devices in a mesh: bx: 16 (over x, y_lo, core), by: 8 (over y_hi, z).
Axes of the slice: x: 4, y: 4 (y_hi: 2, y_lo: 2; y = y_hi * 2 + y_lo), z: 4, core: 2. Of those that a mesh axis runs over, the one named last changes fastest.
Arguments:
- coeffs: bfloat16 [2, 4096, 16, 8, 256], P(None, None, 'bx', 'by'), may hold values from -6 to 6
- interp: bfloat16 [8, 2, 2, 256, 256], replicated, may hold values from -0.25 to 0.25
- src_grid: int32 [256], replicated, may hold values from 0 to 4095
- tgt_grid: int32 [8, 16, 8], replicated, may hold values from 0 to 4095
Outputs:
- result: bfloat16 [2, 4096, 16, 8, 256], P(None, None, 'bx', 'by')
All inputs are finite; a program needn't handle non-finite values.
Results may differ from a plain program's by a relative error of at most 0.02.
Values may be sent and summed in bfloat16 or wider, within the bound.
A program may use at most 128 MiB of HBM per device.

v0:
```python
import math

import jax
import jax.numpy as jnp
from jax import lax
from jax.sharding import PartitionSpec as P

GRID = 4096
LEVELS = 8


def partner_2(shard, axis, stride):
    return lax.ppermute(shard, axis, [(i, i ^ 1 << stride) for i in range(lax.axis_size(axis))])


def apply_mat(state, matrix):
    flat = state.reshape(-1, state.shape[-1])
    return jnp.dot(flat, matrix, preferred_element_type=jnp.float32).reshape(state.shape)


def rotate(total, tgt_value, src_grid):
    prod = tgt_value * src_grid % GRID
    theta = 2.0 * math.pi / GRID * prod.astype(jnp.float32)
    cosine = jnp.cos(theta)
    sine = jnp.sin(theta)
    real_new = total[0] * cosine - total[1] * sine
    imag_new = total[0] * sine + total[1] * cosine
    return jnp.stack([real_new, imag_new]).astype(jnp.bfloat16)


def combine(own, other, weights, child):
    return apply_mat(own, weights[child, child]) + apply_mat(other, weights[child, 1 - child])


def pair_raw(state, level, bit):
    if level % 2 == 0:
        return partner_2(state, "bx", bit)
    return partner_2(state, "by", bit)


def local(coeffs, interp, src_grid, tgt_grid):
    rows = coeffs.shape[1]
    width = coeffs.shape[-1]
    state = coeffs.reshape(2, rows, width)
    pos_x = lax.axis_index("bx")
    pos_y = lax.axis_index("by")
    bits_x = lax.axis_size("bx").bit_length() - 1
    bits_y = lax.axis_size("by").bit_length() - 1
    for level in range(LEVELS):
        if level % 2 == 0:
            bit = level // 2 % bits_x
            place = pos_x
        else:
            bit = level // 2 % bits_y
            place = pos_y
        child = place >> bit & 1
        partner = pair_raw(state, level, bit)
        total = combine(state, partner, interp[level], child)
        state = rotate(total, tgt_grid[level, pos_x, pos_y], src_grid)
    return state.reshape(2, rows, 1, 1, width)


def solution(mesh):
    placed = (P(None, None, "bx", "by", None), P(), P(), P())
    return jax.shard_map(
        local,
        mesh=mesh,
        in_specs=placed,
        out_specs=P(None, None, "bx", "by", None),
        check_vma=False,
    )
```

profile of v0, /device:TPU:1, one launch (start us, length us, event | category | flops | bytes accessed | tf_op | source)
XLA Modules:
  0.0 704.9 jit_solution(12873580879071398903)
XLA Ops:
  0.0 1.4 collective-permute-start
  1.4 1.5 constant_dynamic-slice_fusion.1
  2.9 5.8 fusion.83
  8.7 3.8 fusion.99
  12.5 1.3 fusion.25
  13.9 3.5 fusion
  17.4 1.3 subtract_convert_fusion.7
  18.7 2.6 pad_maximum_fusion
  21.4 1.7 collective-permute-start.1
  23.2 3.1 fusion.22
  26.3 88.1 %collective-permute-done.1 = bf16[2,4096,256]{1,2,0:T(8,128)(2,1)} collective-permute-done((bf16[2,4096,256]{1,2,0:T(8,128)(2,1)}, bf16[2,4096,256]{1,2,0:T(8,128)(2,1)}, u32[]{:S(2)}, u32[]{:S(2)}) %collective-permute-start.1) | collective-permute-done | bytes 4194336 | tf_op jit(solution)/shard_map/ppermute | solution.py:13
  114.4 3.8 convolution_add_fusion.7
  118.2 1.4 subtract_convert_fusion.6
  119.6 2.6 pad_maximum_fusion.1
  122.3 1.2 collective-permute-start.2
  123.5 2.8 fusion.19
  126.4 87.7 %collective-permute-done.2 = bf16[2,4096,256]{2,1,0:T(8,128)(2,1)} collective-permute-done((bf16[2,4096,256]{2,1,0:T(8,128)(2,1)}, bf16[2,4096,256]{2,1,0:T(8,128)(2,1)}, u32[]{:S(2)}, u32[]{:S(2)}) %collective-permute-start.2) | collective-permute-done | bytes 4194336 | tf_op jit(solution)/shard_map/ppermute | solution.py:13
  214.1 3.6 convolution_add_fusion.6
  217.7 1.4 subtract_convert_fusion.5
  219.1 2.6 pad_maximum_fusion.2
  221.8 3.0 collective-permute-start.3
  224.9 2.9 fusion.16
  227.7 86.6 %collective-permute-done.3 = bf16[2,4096,256]{2,1,0:T(8,128)(2,1)} collective-permute-done((bf16[2,4096,256]{2,1,0:T(8,128)(2,1)}, bf16[2,4096,256]{2,1,0:T(8,128)(2,1)}, u32[]{:S(2)}, u32[]{:S(2)}) %collective-permute-start.3) | collective-permute-done | bytes 4194336 | tf_op jit(solution)/shard_map/ppermute | solution.py:13
  314.4 3.6 convolution_add_fusion.5
  318.0 1.4 subtract_convert_fusion.4
  319.4 2.6 pad_maximum_fusion.3
  322.1 1.2 collective-permute-start.4
  323.3 2.9 fusion.13
  326.2 86.0 %collective-permute-done.4 = bf16[2,4096,256]{2,1,0:T(8,128)(2,1)} collective-permute-done((bf16[2,4096,256]{2,1,0:T(8,128)(2,1)}, bf16[2,4096,256]{2,1,0:T(8,128)(2,1)}, u32[]{:S(2)}, u32[]{:S(2)}) %collective-permute-start.4) | collective-permute-done | bytes 4194336 | tf_op jit(solution)/shard_map/ppermute | solution.py:13
  412.1 3.6 convolution_add_fusion.4
  415.7 1.2 subtract_convert_fusion.3
  416.9 2.6 pad_maximum_fusion.4
  419.6 2.9 collective-permute-start.5
  422.6 2.8 fusion.10
  425.4 84.8 %collective-permute-done.5 = bf16[2,4096,256]{2,1,0:T(8,128)(2,1)} collective-permute-done((bf16[2,4096,256]{2,1,0:T(8,128)(2,1)}, bf16[2,4096,256]{2,1,0:T(8,128)(2,1)}, u32[]{:S(2)}, u32[]{:S(2)}) %collective-permute-start.5) | collective-permute-done | bytes 4194336 | tf_op jit(solution)/shard_map/ppermute | solution.py:13
  510.3 3.6 convolution_add_fusion.3
  513.9 1.2 subtract_convert_fusion.2
  515.0 2.6 pad_maximum_fusion.5
  517.7 2.7 collective-permute-start.6
  520.5 2.9 fusion.7
  523.4 84.1 %collective-permute-done.6 = bf16[2,4096,256]{2,1,0:T(8,128)(2,1)} collective-permute-done((bf16[2,4096,256]{2,1,0:T(8,128)(2,1)}, bf16[2,4096,256]{2,1,0:T(8,128)(2,1)}, u32[]{:S(2)}, u32[]{:S(2)}) %collective-permute-start.6) | collective-permute-done | bytes 4194336 | tf_op jit(solution)/shard_map/ppermute | solution.py:13
  607.5 3.6 convolution_add_fusion.2
  611.1 1.4 subtract_convert_fusion.1
  613.0 1.3 fusion.4
  614.2 85.7 %collective-permute-done.7 = bf16[2,4096,256]{2,1,0:T(8,128)(2,1)S(1)} collective-permute-done((bf16[2,4096,256]{2,1,0:T(8,128)(2,1)S(1)}, bf16[2,4096,256]{2,1,0:T(8,128)(2,1)S(1)}, u32[]{:S(2)}, u32[]{:S(2)}) %collective-permute-start.7) | collective-permute-done | bytes 4194336 | tf_op jit(solution)/shard_map/ppermute | solution.py:13
  699.9 1.3 convolution_add_fusion.1
  701.2 1.4 fusion.1
  702.5 2.4 pad_maximum_fusion.7
  (25 shorter events, 1.4 us)
Async XLA Ops:
  0.0 13.9 %collective-permute-start = (bf16[2,4096,256]{2,1,0:T(8,128)(2,1)}, bf16[2,4096,256]{2,1,0:T(8,128)(2,1)}, u32[]{:S(2)}, u32[]{:S(2)}) collective-permute-start(bf16[2,4096,256]{2,1,0:T(8,128)(2,1)} %bitcast.114), channel_id=1, source_target_pairs={{0,8},{8,0},{16,24},{24,16},{32,40},{40,32},{48,56},{56,48},{64,72... | collective-permute-start | bytes 12582920 | tf_op jit(solution)/shard_map/ppermute | solution.py:13
  8.7 3.9 copy-start.6
  18.7 2.7 copy-start.2
  21.4 93.0 %collective-permute-start.1 = (bf16[2,4096,256]{1,2,0:T(8,128)(2,1)}, bf16[2,4096,256]{1,2,0:T(8,128)(2,1)}, u32[]{:S(2)}, u32[]{:S(2)}) collective-permute-start(bf16[2,4096,256]{1,2,0:T(8,128)(2,1)} %pad_maximum_fusion), channel_id=1, source_target_pairs={{0,1},{1,0},{2,3},{3,2},{4,5},{5,4},{6,7},{7,6},{8,9},{9,8},{10,11... | collective-permute-start | bytes 12582920 | tf_op jit(solution)/shard_map/ppermute | solution.py:13
  119.6 2.7 copy-start.3
  122.3 91.8 %collective-permute-start.2 = (bf16[2,4096,256]{2,1,0:T(8,128)(2,1)}, bf16[2,4096,256]{2,1,0:T(8,128)(2,1)}, u32[]{:S(2)}, u32[]{:S(2)}) collective-permute-start(bf16[2,4096,256]{2,1,0:T(8,128)(2,1)} %pad_maximum_fusion.1), channel_id=1, source_target_pairs={{0,16},{8,24},{16,0},{24,8},{32,48},{40,56},{48,32},{56,40},{64,80... | collective-permute-start | bytes 12582920 | tf_op jit(solution)/shard_map/ppermute | solution.py:13
  219.1 2.7 copy-start.4
  221.8 92.6 %collective-permute-start.3 = (bf16[2,4096,256]{2,1,0:T(8,128)(2,1)}, bf16[2,4096,256]{2,1,0:T(8,128)(2,1)}, u32[]{:S(2)}, u32[]{:S(2)}) collective-permute-start(bf16[2,4096,256]{2,1,0:T(8,128)(2,1)} %pad_maximum_fusion.2), channel_id=1, source_target_pairs={{0,2},{1,3},{2,0},{3,1},{4,6},{5,7},{6,4},{7,5},{8,10},{9,11},{10,... | collective-permute-start | bytes 12582920 | tf_op jit(solution)/shard_map/ppermute | solution.py:13
  319.4 2.7 copy-start.5
  322.1 90.1 %collective-permute-start.4 = (bf16[2,4096,256]{2,1,0:T(8,128)(2,1)}, bf16[2,4096,256]{2,1,0:T(8,128)(2,1)}, u32[]{:S(2)}, u32[]{:S(2)}) collective-permute-start(bf16[2,4096,256]{2,1,0:T(8,128)(2,1)} %pad_maximum_fusion.3), channel_id=1, source_target_pairs={{0,32},{8,40},{16,48},{24,56},{32,0},{40,8},{48,16},{56,24},{64,96... | collective-permute-start | bytes 12582920 | tf_op jit(solution)/shard_map/ppermute | solution.py:13
  416.9 2.7 copy-start.1
  419.6 90.6 %collective-permute-start.5 = (bf16[2,4096,256]{2,1,0:T(8,128)(2,1)}, bf16[2,4096,256]{2,1,0:T(8,128)(2,1)}, u32[]{:S(2)}, u32[]{:S(2)}) collective-permute-start(bf16[2,4096,256]{2,1,0:T(8,128)(2,1)} %pad_maximum_fusion.4), channel_id=1, source_target_pairs={{0,4},{1,5},{2,6},{3,7},{4,0},{5,1},{6,2},{7,3},{8,12},{9,13},{10,... | collective-permute-start | bytes 12582920 | tf_op jit(solution)/shard_map/ppermute | solution.py:13
  515.0 2.7 copy-start
  517.7 89.7 %collective-permute-start.6 = (bf16[2,4096,256]{2,1,0:T(8,128)(2,1)}, bf16[2,4096,256]{2,1,0:T(8,128)(2,1)}, u32[]{:S(2)}, u32[]{:S(2)}) collective-permute-start(bf16[2,4096,256]{2,1,0:T(8,128)(2,1)} %pad_maximum_fusion.5), channel_id=1, source_target_pairs={{0,64},{8,72},{16,80},{24,88},{32,96},{40,104},{48,112},{56,120},{... | collective-permute-start | bytes 12582920 | tf_op jit(solution)/shard_map/ppermute | solution.py:13
  612.8 87.1 %collective-permute-start.7 = (bf16[2,4096,256]{2,1,0:T(8,128)(2,1)S(1)}, bf16[2,4096,256]{2,1,0:T(8,128)(2,1)S(1)}, u32[]{:S(2)}, u32[]{:S(2)}) collective-permute-start(bf16[2,4096,256]{2,1,0:T(8,128)(2,1)S(1)} %pad_maximum_fusion.6), channel_id=1, source_target_pairs={{0,1},{1,0},{2,3},{3,2},{4,5},{5,4},{6,7},{7,6},{8,9},{9,8},{10,11... | collective-permute-start | bytes 12582920 | tf_op jit(solution)/shard_map/ppermute | solution.py:13
where the time goes:
time: 710 us; the launch traced here: 705 us
  waiting for transfers between devices  603 us (85%)
  matrix products  46.6 us (7%)
  other arithmetic  34.6 us (5%)
  starting transfers between devices  14.4 us (2%)
    ppermute x8, waiting for transfers between devices, partner_2(): lax.ppermute(shard, axis, [(i, i ^ 1 << stride) for i in range(lax.axis_s...  603 us
    dot_general x16, matrix products, apply_mat(): jnp.dot(flat, matrix, preferred_element_type=jnp.float32)  46.6 us
    another operation x9, other arithmetic, rotate(): return jnp.stack([real_new, imag_new]).astype(jnp.bfloat16)  19.7 us
    ppermute x8, starting transfers between devices, partner_2(): lax.ppermute(shard, axis, [(i, i ^ 1 << stride) for i in range(lax.axis_s...  14.4 us
  transfers between devices with their start and end apart: 8, of which 7 were waited for; matrix products, arithmetic and copies ran while one was open for 4% of the time, Pallas kernels for 0%

commit v1 on v0

v1 whole, which is shorter than its diff:
```python
import functools
import math

import jax
import jax.numpy as jnp
from jax import lax
from jax.experimental import pallas as pl
from jax.experimental.pallas import tpu as pltpu
from jax.sharding import PartitionSpec as P

GRID = 4096
LEVELS = 8
CHUNKS = 2
GROUP = 32
PAIRS = 16
SIDE = 4
BATCH = SIDE * SIDE
BATCHES = 2 * SIDE
EARLY = 6
MESH = pl.DeviceIdType.MESH


def level_bits(n_bx, n_by):
    bits_x = n_bx.bit_length() - 1
    bits_y = n_by.bit_length() - 1
    bits = []
    for level in range(LEVELS):
        if level % 2 == 0:
            bits.append(bits_y + level // 2 % bits_x)
        else:
            bits.append(level // 2 % bits_y)
    return bits


def phases(prod):
    quadrant = (prod + GRID // 8) >> 10
    angle = (prod - (quadrant << 10)).astype(jnp.float32) * (2.0 * math.pi / GRID)
    sq = angle * angle
    cosine = 1.0 + sq * (-1 / 2 + sq * (1 / 24 + sq * (-1 / 720 + sq * (1 / 40320))))
    sine = angle * (1.0 + sq * (-1 / 6 + sq * (1 / 120 + sq * (-1 / 5040 + sq * (1 / 362880)))))
    odd = (quadrant & 1) == 1
    first = jnp.where(odd, sine, cosine)
    second = jnp.where(odd, cosine, sine)
    cos_sign = jnp.where((quadrant == 1) | (quadrant == 2), -1.0, 1.0)
    sin_sign = jnp.where((quadrant == 2) | (quadrant == 3), -1.0, 1.0)
    return first * cos_sign, second * sin_sign


def apply_level(level, bit, source, target, interp, cosine, sine):
    boxes, _, rows, width = source.shape
    stride = 1 << bit
    weights = [interp[level, child].reshape(2 * width, width) for child in range(2)]
    weights = jnp.concatenate(weights, axis=1)

    def body(group, carry):
        if stride <= GROUP:
            low = [group * (2 * GROUP) + (i // stride * 2 * stride + i % stride) for i in range(GROUP)]
        else:
            runs = stride // GROUP
            base = group // runs * (2 * stride) + group % runs * GROUP
            low = [base + i for i in range(GROUP)]
        for begin in range(0, GROUP, PAIRS):
            some = low[begin:begin + PAIRS]
            halves = []
            for child in range(2):
                parts = [source[box + child * stride].reshape(2 * rows, width) for box in some]
                halves.append(jnp.concatenate(parts, axis=0))
            operand = jnp.concatenate(halves, axis=1)
            total = jnp.dot(operand, weights, preferred_element_type=jnp.float32)
            for i, box in enumerate(some):
                for child in range(2):
                    here = box + child * stride
                    re = total[2 * i * rows:(2 * i + 1) * rows, child * width:(child + 1) * width]
                    im = total[(2 * i + 1) * rows:(2 * i + 2) * rows, child * width:(child + 1) * width]
                    c = cosine[level, pl.ds(here, 1), :]
                    s = sine[level, pl.ds(here, 1), :]
                    target[here, 0] = (re * c - im * s).astype(jnp.bfloat16)
                    target[here, 1] = (re * s + im * c).astype(jnp.bfloat16)
        return carry

    lax.fori_loop(0, boxes // 2 // GROUP, body, 0)


def kernel(
    n_bx, n_by, coeffs, interp_hbm, tgt_hbm, src_hbm, out,
    state, spare, interp, tgt, src, cosine, sine, in_send, in_recv, out_send, out_recv, load_sem,
):
    boxes = n_bx * n_by
    share = state.shape[3]
    bits = level_bits(n_bx, n_by)
    my_bx, my_by = lax.axis_index("bx"), lax.axis_index("by")
    me = my_bx * n_by + my_by
    my_x = my_bx // 4
    my_y = my_by // 4 * 2 + my_bx // 2 % 2
    my_z = my_by % 4
    my_core = my_bx % 2

    loads = [
        pltpu.make_async_copy(src_hbm, src, load_sem.at[0]),
        pltpu.make_async_copy(tgt_hbm, tgt, load_sem.at[1]),
        pltpu.make_async_copy(interp_hbm, interp, load_sem.at[2]),
    ]
    for load in loads:
        load.start()

    sign = 1 + (SIDE - 2) * my_core
    xs = [(my_x + sign * i) % SIDE * 4 for i in range(SIDE)]
    ys = [(my_y + sign * i) % SIDE for i in range(SIDE)]
    ys_bx = [y % 2 * 2 for y in ys]
    ys_by = [y // 2 * 4 for y in ys]

    def batch(number, visit):
        core = (my_core + number // SIDE) % 2
        bys = [ys_by[i] + (my_z + sign * (number + i)) % SIDE for i in range(SIDE)]
        for second in range(SIDE):
            for first in range(SIDE):
                if isinstance(number, int) and number == first == second == 0:
                    continue
                i = (first + second) % SIDE
                visit(xs[first] + ys_bx[i] + core, bys[i])

    def batches(start, stop, visit):
        if start == 0:
            batch(0, functools.partial(visit, 0))
            start = 1

        def body(number, carry):
            batch(number, functools.partial(visit, number))
            return carry

        lax.fori_loop(start, stop, body, 0)

    def rows_of(chunk, box):
        return pl.ds(pl.multiple_of((chunk * boxes + box) * share, share), share)

    def greet(number, bx, by):
        pl.semaphore_signal(barrier, inc=1, device_id=(bx, by), device_id_type=MESH)

    def scatter(chunk, number, bx, by):
        pltpu.make_async_remote_copy(
            src_ref=coeffs.at[:, rows_of(chunk, bx * n_by + by)],
            dst_ref=state.at[chunk, me],
            send_sem=in_send.at[chunk, number],
            recv_sem=in_recv.at[chunk],
            device_id=(bx, by),
            device_id_type=MESH,
        ).start()

    def give_back(chunk, number, bx, by):
        pltpu.make_async_remote_copy(
            src_ref=state.at[chunk, bx * n_by + by],
            dst_ref=out.at[:, rows_of(chunk, me)],
            send_sem=out_send.at[chunk],
            recv_sem=out_recv.at[chunk],
            device_id=(bx, by),
            device_id_type=MESH,
        ).start()

    def wait_sent(chunk, number, count):
        sent = state.at[chunk, pl.ds(0, count)]
        pltpu.make_async_copy(sent, sent, in_send.at[chunk, number]).wait()

    barrier = pltpu.get_barrier_semaphore()
    batches(0, BATCHES, greet)
    pl.semaphore_wait(barrier, boxes - 1)

    batches(0, BATCHES, functools.partial(scatter, 0))
    for chunk in range(CHUNKS):
        pltpu.make_async_copy(coeffs.at[:, rows_of(chunk, me)], state.at[chunk, me], in_recv.at[chunk]).start()

    for load in loads:
        load.wait()

    def tables(level, carry):
        columns = tgt[level]
        for bx in range(n_bx):
            prod = (columns[:, bx:bx + 1] * src[...]) & (GRID - 1)
            here = pl.ds(bx * n_by, n_by)
            cosine[level, here, :], sine[level, here, :] = phases(prod)
        return carry

    lax.fori_loop(0, LEVELS, tables, 0)

    for number in range(EARLY):
        wait_sent(0, number, BATCH - (number == 0))
    batches(0, BATCHES // 2, functools.partial(scatter, 1))
    for number in range(EARLY, BATCHES):
        wait_sent(0, number, BATCH)
    batches(BATCHES // 2, BATCHES, functools.partial(scatter, 1))

    def work(chunk, carry):
        pltpu.make_async_copy(state.at[chunk], state.at[chunk], in_recv.at[chunk]).wait()

        for level in range(LEVELS):
            buffers = (state.at[chunk], spare)
            apply_level(level, bits[level], buffers[level % 2], buffers[1 - level % 2], interp, cosine, sine)
        pltpu.make_async_copy(state.at[chunk, me], out.at[:, rows_of(chunk, me)], out_recv.at[chunk]).start()
        batches(0, BATCHES, functools.partial(give_back, chunk))
        return carry

    lax.fori_loop(0, CHUNKS, work, 0)

    for number in range(BATCHES):
        wait_sent(1, number, BATCH - (number == 0))
    for chunk in range(CHUNKS):
        whole = out.at[:, pl.ds(chunk * boxes * share, boxes * share)]
        pltpu.make_async_copy(whole, whole, out_recv.at[chunk]).wait()
        others = state.at[chunk, pl.ds(0, boxes - 1)]
        pltpu.make_async_copy(others, others, out_send.at[chunk]).wait()


def local(n_bx, n_by, coeffs, interp, src_grid, tgt_grid):
    rows, width = coeffs.shape[1], coeffs.shape[-1]
    boxes = n_bx * n_by
    share = rows // boxes // CHUNKS
    anywhere = pl.BlockSpec(memory_space=pl.ANY)
    hbm = pl.BlockSpec(memory_space=pltpu.HBM)
    table = pltpu.VMEM((LEVELS, boxes, width), jnp.float32)
    dma = pltpu.SemaphoreType.DMA
    result = pl.pallas_call(
        functools.partial(kernel, n_bx, n_by),
        out_shape=jax.ShapeDtypeStruct((2, rows, width), coeffs.dtype),
        in_specs=[hbm] * 4,
        out_specs=anywhere,
        scratch_shapes=[
            pltpu.VMEM((CHUNKS, boxes, 2, share, width), coeffs.dtype),
            pltpu.VMEM((boxes, 2, share, width), coeffs.dtype),
            pltpu.VMEM(interp.shape, interp.dtype),
            pltpu.VMEM((LEVELS, n_by, n_bx), jnp.int32),
            pltpu.VMEM((1, width), jnp.int32),
            table,
            table,
            dma((CHUNKS, BATCHES)),
            dma((CHUNKS,)),
            dma((CHUNKS,)),
            dma((CHUNKS,)),
            dma((3,)),
        ],
        compiler_params=pltpu.CompilerParams(
            collective_id=0, has_side_effects=True, vmem_limit_bytes=48 * 1024 * 1024
        ),
        cost_estimate=pl.CostEstimate(
            flops=4 * LEVELS * coeffs.size * width, bytes_accessed=16 * 2**20, transcendentals=0
        ),
        name="butterfly",
    )(
        coeffs.reshape(2, rows, width),
        interp,
        pltpu.with_memory_space_constraint(tgt_grid.transpose(0, 2, 1), pltpu.HBM),
        pltpu.with_memory_space_constraint(src_grid.reshape(1, width), pltpu.HBM),
    )
    return result.reshape(2, rows, 1, 1, width)


def solution(mesh):
    placed = (P(None, None, "bx", "by", None), P(), P(), P())
    return jax.shard_map(
        functools.partial(local, mesh.shape["bx"], mesh.shape["by"]),
        mesh=mesh,
        in_specs=placed,
        out_specs=P(None, None, "bx", "by", None),
        check_vma=False,
    )
```

time: 710 us -> 106 us (0.15)
  waiting for transfers between devices: 603 us -> 0 us
  Pallas kernels: 0 us -> 104 us
  matrix products: 46.6 us -> 0 us
  other arithmetic: 34.6 us -> 0 us
  starting transfers between devices: 14.4 us -> 0 us
    ppermute x8 -> x0, waiting for transfers between devices: 603 us -> none  [partner_2(): lax.ppermute(shard, axis, [(i, i ^ 1 << stride) for i in range(lax.axis_s...]
    pallas_call x0 -> x1, Pallas kernels: none -> 104 us  [local(): pl.pallas_call(functools.partial(kernel, n_bx, n_by), out_shape=jax.Shape...]
    dot_general x16 -> x0, matrix products: 46.6 us -> none  [apply_mat(): jnp.dot(flat, matrix, preferred_element_type=jnp.float32)]
    another operation x16 -> x0, other arithmetic: 28.8 us -> none  [the longest x9 19.7 us: rotate(): return jnp.stack([real_new, imag_new]).astype(jnp.bfloat16)]
    ppermute x8 -> x0, starting transfers between devices: 14.4 us -> none  [partner_2(): lax.ppermute(shard, axis, [(i, i ^ 1 << stride) for i in range(lax.axis_s...]
  transfers between devices with their start and end apart: 8 -> 0, of which waited for: 7 -> 0; matrix products, arithmetic and copies ran while one was open for 4% -> 0% of each run, Pallas kernels for 0% -> 0%
where the time goes in v1:
time: 106 us
  Pallas kernels  104 us (98%)
  local copies, waits for them, and re-layouts  2.02 us (2%)
    pallas_call x1, Pallas kernels, local(): pl.pallas_call(functools.partial(kernel, n_bx, n_by), out_shape=jax.Shape...  104 us

profile of v1, /device:TPU:1, one launch (start us, length us, event | category | flops | bytes accessed | tf_op | source)
XLA Modules:
  0.0 106.1 jit_solution(12173206751089492042)
XLA Ops:
  0.0 104.1 %butterfly.1 = bf16[2,4096,256]{2,1,0:T(8,128)(2,1)S(1)} custom-call(bf16[2,4096,256]{2,1,0:T(8,128)(2,1)} %bitcast.7, bf16[8,2,2,256,256]{4,3,2,1,0:T(8,128)(2,1)} %interp_hbm.1, s32[8,8,16]{2,1,0:T(8,128)} %bitcast.8, s32[1,256]{1,0:T(1,128)} %bitcast.9), custom_call_target="tpu_custom_call" | custom-call | flops 17179869184 | bytes 16777216 | tf_op jit(solution)/shard_map/butterfly/pallas_call | solution.py:220
  104.1 2.0 %copy.7 = bf16[2,4096,1,1,256]{4,1,3,2,0:T(8,128)(2,1)} copy(bf16[2,4096,1,1,256]{4,1,3,2,0:T(8,128)(2,1)S(1)} %bitcast.6) | data formatting | bytes 8388608

commit v2 on v1

--- a/solution.py
+++ b/solution.py
@@ -103,21 +103,23 @@
     for load in loads:
         load.start()
 
-    sign = 1 + (SIDE - 2) * my_core
-    xs = [(my_x + sign * i) % SIDE * 4 for i in range(SIDE)]
-    ys = [(my_y + sign * i) % SIDE for i in range(SIDE)]
+    ahead = SIDE // 2 * my_core
+    xs = [(my_x + ahead + i) % SIDE * 4 for i in range(SIDE)]
+    ys = [(my_y + ahead + i) % SIDE for i in range(SIDE)]
     ys_bx = [y % 2 * 2 for y in ys]
     ys_by = [y // 2 * 4 for y in ys]
 
     def batch(number, visit):
         core = (my_core + number // SIDE) % 2
-        bys = [ys_by[i] + (my_z + sign * (number + i)) % SIDE for i in range(SIDE)]
+        bys = [ys_by[i] + (my_z + ahead + number + i) % SIDE for i in range(SIDE)]
         for second in range(SIDE):
             for first in range(SIDE):
-                if isinstance(number, int) and number == first == second == 0:
-                    continue
                 i = (first + second) % SIDE
-                visit(xs[first] + ys_bx[i] + core, bys[i])
+                send = functools.partial(visit, xs[first] + ys_bx[i] + core, bys[i])
+                if isinstance(number, int) and number == second == 0 and first % 2 == 0:
+                    pl.when(my_core != first // 2)(send)
+                else:
+                    send()
 
     def batches(start, stop, visit):
         if start == 0:

time: 106 us -> 106 us (level)
  no operation moved by 1% of the time
where the time goes in v2:
time: 106 us
  Pallas kernels  104 us (98%)
  local copies, waits for them, and re-layouts  2.02 us (2%)
    pallas_call x1, Pallas kernels, local(): pl.pallas_call(functools.partial(kernel, n_bx, n_by), out_shape=jax.Shape...  104 us

profile of v2, /device:TPU:1, one launch (start us, length us, event | category | flops | bytes accessed | tf_op | source)
XLA Modules:
  0.0 106.3 jit_solution(11323071676393114488)
XLA Ops:
  0.0 104.3 %butterfly.1 = bf16[2,4096,256]{2,1,0:T(8,128)(2,1)S(1)} custom-call(bf16[2,4096,256]{2,1,0:T(8,128)(2,1)} %bitcast.7, bf16[8,2,2,256,256]{4,3,2,1,0:T(8,128)(2,1)} %interp_hbm.1, s32[8,8,16]{2,1,0:T(8,128)} %bitcast.8, s32[1,256]{1,0:T(1,128)} %bitcast.9), custom_call_target="tpu_custom_call" | custom-call | flops 17179869184 | bytes 16777216 | tf_op jit(solution)/shard_map/butterfly/pallas_call | solution.py:222
  104.3 2.0 %copy.7 = bf16[2,4096,1,1,256]{4,1,3,2,0:T(8,128)(2,1)} copy(bf16[2,4096,1,1,256]{4,1,3,2,0:T(8,128)(2,1)S(1)} %bitcast.6) | data formatting | bytes 8388608

commit v3 on v1

--- a/solution.py
+++ b/solution.py
@@ -83,7 +83,7 @@
 
 def kernel(
     n_bx, n_by, coeffs, interp_hbm, tgt_hbm, src_hbm, out,
-    state, spare, interp, tgt, src, cosine, sine, in_send, in_recv, out_send, out_recv, load_sem,
+    state, spare, interp, tgt, src, cosine, sine, in_send, in_recv, out_send, out_recv, load_sem, heard,
 ):
     boxes = n_bx * n_by
     share = state.shape[3]
@@ -100,8 +100,16 @@
         pltpu.make_async_copy(tgt_hbm, tgt, load_sem.at[1]),
         pltpu.make_async_copy(interp_hbm, interp, load_sem.at[2]),
     ]
+    barrier = pltpu.get_barrier_semaphore()
+    across = [((my_bx + i) % n_bx, my_by) for i in range(1, n_bx)]
+    along = [(my_bx, (my_by + i) % n_by) for i in range(1, n_by)]
+    for device in along + across:
+        pl.semaphore_signal(barrier, inc=1, device_id=device, device_id_type=MESH)
     for load in loads:
         load.start()
+    pl.semaphore_wait(barrier, len(along) + len(across))
+    for device in across:
+        pl.semaphore_signal(heard, inc=1, device_id=device, device_id_type=MESH)
 
     sign = 1 + (SIDE - 2) * my_core
     xs = [(my_x + sign * i) % SIDE * 4 for i in range(SIDE)]
@@ -133,9 +141,6 @@
     def rows_of(chunk, box):
         return pl.ds(pl.multiple_of((chunk * boxes + box) * share, share), share)
 
-    def greet(number, bx, by):
-        pl.semaphore_signal(barrier, inc=1, device_id=(bx, by), device_id_type=MESH)
-
     def scatter(chunk, number, bx, by):
         pltpu.make_async_remote_copy(
             src_ref=coeffs.at[:, rows_of(chunk, bx * n_by + by)],
@@ -160,10 +165,7 @@
         sent = state.at[chunk, pl.ds(0, count)]
         pltpu.make_async_copy(sent, sent, in_send.at[chunk, number]).wait()
 
-    barrier = pltpu.get_barrier_semaphore()
-    batches(0, BATCHES, greet)
-    pl.semaphore_wait(barrier, boxes - 1)
-
+    pl.semaphore_wait(heard, len(across))
     batches(0, BATCHES, functools.partial(scatter, 0))
     for chunk in range(CHUNKS):
         pltpu.make_async_copy(coeffs.at[:, rows_of(chunk, me)], state.at[chunk, me], in_recv.at[chunk]).start()
@@ -235,6 +237,7 @@
             dma((CHUNKS,)),
             dma((CHUNKS,)),
             dma((3,)),
+            pltpu.SemaphoreType.REGULAR,
         ],
         compiler_params=pltpu.CompilerParams(
             collective_id=0, has_side_effects=True, vmem_limit_bytes=48 * 1024 * 1024

time: 106 us -> 107 us (level)
  no operation moved by 1% of the time
where the time goes in v3:
time: 107 us
  Pallas kernels  105 us (98%)
  local copies, waits for them, and re-layouts  2.02 us (2%)
    pallas_call x1, Pallas kernels, local(): pl.pallas_call(functools.partial(kernel, n_bx, n_by), out_shape=jax.Shape...  105 us

profile of v3, /device:TPU:1, one launch (start us, length us, event | category | flops | bytes accessed | tf_op | source)
XLA Modules:
  0.0 106.6 jit_solution(3572235494197152200)
XLA Ops:
  0.0 104.6 %butterfly.1 = bf16[2,4096,256]{2,1,0:T(8,128)(2,1)S(1)} custom-call(bf16[2,4096,256]{2,1,0:T(8,128)(2,1)} %bitcast.7, bf16[8,2,2,256,256]{4,3,2,1,0:T(8,128)(2,1)} %interp_hbm.1, s32[8,8,16]{2,1,0:T(8,128)} %bitcast.8, s32[1,256]{1,0:T(1,128)} %bitcast.9), custom_call_target="tpu_custom_call" | custom-call | flops 17179869184 | bytes 16777216 | tf_op jit(solution)/shard_map/butterfly/pallas_call | solution.py:222
  104.6 2.0 %copy.7 = bf16[2,4096,1,1,256]{4,1,3,2,0:T(8,128)(2,1)} copy(bf16[2,4096,1,1,256]{4,1,3,2,0:T(8,128)(2,1)S(1)} %bitcast.6) | data formatting | bytes 8388608

commit v4 on v3

--- a/solution.py
+++ b/solution.py
@@ -83,7 +83,7 @@
 
 def kernel(
     n_bx, n_by, coeffs, interp_hbm, tgt_hbm, src_hbm, out,
-    state, spare, interp, tgt, src, cosine, sine, in_send, in_recv, out_send, out_recv, load_sem, heard,
+    staged, state, spare, interp, tgt, src, cosine, sine, in_send, in_recv, out_send, out_recv, load_sem, stage_sem, heard,
 ):
     boxes = n_bx * n_by
     share = state.shape[3]
@@ -100,12 +100,21 @@
         pltpu.make_async_copy(tgt_hbm, tgt, load_sem.at[1]),
         pltpu.make_async_copy(interp_hbm, interp, load_sem.at[2]),
     ]
+    halves = [
+        pltpu.make_async_copy(
+            coeffs.at[:, pl.ds(chunk * boxes * share, boxes * share)],
+            staged.at[:, pl.ds(chunk * boxes * share, boxes * share)],
+            stage_sem.at[chunk],
+        )
+        for chunk in range(CHUNKS)
+    ]
+
     barrier = pltpu.get_barrier_semaphore()
     across = [((my_bx + i) % n_bx, my_by) for i in range(1, n_bx)]
     along = [(my_bx, (my_by + i) % n_by) for i in range(1, n_by)]
     for device in along + across:
         pl.semaphore_signal(barrier, inc=1, device_id=device, device_id_type=MESH)
-    for load in loads:
+    for load in halves + loads:
         load.start()
     pl.semaphore_wait(barrier, len(along) + len(across))
     for device in across:
@@ -125,7 +134,7 @@
                 if isinstance(number, int) and number == first == second == 0:
                     continue
                 i = (first + second) % SIDE
-                visit(xs[first] + ys_bx[i] + core, bys[i])
+                visit(first % 2, xs[first] + ys_bx[i] + core, bys[i])
 
     def batches(start, stop, visit):
         if start == 0:
@@ -141,9 +150,9 @@
     def rows_of(chunk, box):
         return pl.ds(pl.multiple_of((chunk * boxes + box) * share, share), share)
 
-    def scatter(chunk, number, bx, by):
+    def scatter(chunk, number, odd, bx, by):
         pltpu.make_async_remote_copy(
-            src_ref=coeffs.at[:, rows_of(chunk, bx * n_by + by)],
+            src_ref=(staged if odd else coeffs).at[:, rows_of(chunk, bx * n_by + by)],
             dst_ref=state.at[chunk, me],
             send_sem=in_send.at[chunk, number],
             recv_sem=in_recv.at[chunk],
@@ -151,7 +160,7 @@
             device_id_type=MESH,
         ).start()
 
-    def give_back(chunk, number, bx, by):
+    def give_back(chunk, number, odd, bx, by):
         pltpu.make_async_remote_copy(
             src_ref=state.at[chunk, bx * n_by + by],
             dst_ref=out.at[:, rows_of(chunk, me)],
@@ -166,7 +175,9 @@
         pltpu.make_async_copy(sent, sent, in_send.at[chunk, number]).wait()
 
     pl.semaphore_wait(heard, len(across))
+    halves[0].wait()
     batches(0, BATCHES, functools.partial(scatter, 0))
+    halves[1].wait()
     for chunk in range(CHUNKS):
         pltpu.make_async_copy(coeffs.at[:, rows_of(chunk, me)], state.at[chunk, me], in_recv.at[chunk]).start()
 
@@ -225,6 +236,7 @@
         in_specs=[hbm] * 4,
         out_specs=anywhere,
         scratch_shapes=[
+            pltpu.VMEM((2, rows, width), coeffs.dtype),
             pltpu.VMEM((CHUNKS, boxes, 2, share, width), coeffs.dtype),
             pltpu.VMEM((boxes, 2, share, width), coeffs.dtype),
             pltpu.VMEM(interp.shape, interp.dtype),
@@ -237,6 +249,7 @@
             dma((CHUNKS,)),
             dma((CHUNKS,)),
             dma((3,)),
+            dma((CHUNKS,)),
             pltpu.SemaphoreType.REGULAR,
         ],
         compiler_params=pltpu.CompilerParams(

time: 107 us -> 107 us (level)
  no operation moved by 1% of the time
where the time goes in v4:
time: 107 us
  Pallas kernels  104 us (97%)
  local copies, waits for them, and re-layouts  2.02 us (2%)
    pallas_call x1, Pallas kernels, local(): pl.pallas_call(functools.partial(kernel, n_bx, n_by), out_shape=jax.Shape...  104 us

profile of v4, /device:TPU:1, one launch (start us, length us, event | category | flops | bytes accessed | tf_op | source)
XLA Modules:
  0.0 106.5 jit_solution(16751881046270796336)
XLA Ops:
  0.0 104.5 %butterfly.1 = bf16[2,4096,256]{2,1,0:T(8,128)(2,1)S(1)} custom-call(bf16[2,4096,256]{2,1,0:T(8,128)(2,1)} %bitcast.7, bf16[8,2,2,256,256]{4,3,2,1,0:T(8,128)(2,1)} %interp_hbm.1, s32[8,8,16]{2,1,0:T(8,128)} %bitcast.8, s32[1,256]{1,0:T(1,128)} %bitcast.9), custom_call_target="tpu_custom_call" | custom-call | flops 17179869184 | bytes 16777216 | tf_op jit(solution)/shard_map/butterfly/pallas_call | solution.py:233
  104.5 2.0 %copy.7 = bf16[2,4096,1,1,256]{4,1,3,2,0:T(8,128)(2,1)} copy(bf16[2,4096,1,1,256]{4,1,3,2,0:T(8,128)(2,1)S(1)} %bitcast.6) | data formatting | bytes 8388608

commit v5 on v1

--- a/solution.py
+++ b/solution.py
@@ -83,7 +83,7 @@
 
 def kernel(
     n_bx, n_by, coeffs, interp_hbm, tgt_hbm, src_hbm, out,
-    state, spare, interp, tgt, src, cosine, sine, in_send, in_recv, out_send, out_recv, load_sem,
+    state, spare, interp, tgt, src, cosine, sine, in_send, in_recv, out_send, out_recv, load_sem, heard,
 ):
     boxes = n_bx * n_by
     share = state.shape[3]
@@ -100,22 +100,38 @@
         pltpu.make_async_copy(tgt_hbm, tgt, load_sem.at[1]),
         pltpu.make_async_copy(interp_hbm, interp, load_sem.at[2]),
     ]
-    for load in loads:
-        load.start()
-
     sign = 1 + (SIDE - 2) * my_core
     xs = [(my_x + sign * i) % SIDE * 4 for i in range(SIDE)]
     ys = [(my_y + sign * i) % SIDE for i in range(SIDE)]
     ys_bx = [y % 2 * 2 for y in ys]
     ys_by = [y // 2 * 4 for y in ys]
 
-    def batch(number, visit):
+    zs = [(my_z + sign * i) % SIDE for i in range(SIDE)]
+    line = [(xs[i] + ys_bx[0] + (my_core + j) % 2, my_by) for j in range(2) for i in range(SIDE)][1:]
+    plane = [
+        (xs[0] + ys_bx[i] + my_core, ys_by[i] + zs[(i + j) % SIDE]) for j in range(SIDE) for i in range(SIDE)
+    ][1:]
+    barrier = pltpu.get_barrier_semaphore()
+    for device in plane + line:
+        pl.semaphore_signal(barrier, inc=1, device_id=device, device_id_type=MESH)
+    for load in loads:
+        load.start()
+    pl.semaphore_wait(barrier, len(plane) + len(line))
+    for device in line:
+        pl.semaphore_signal(heard, inc=1, device_id=device, device_id_type=MESH)
+
+    def on_line_or_plane(number, first, second):
+        return (number < SIDE and first == 0) or (number % SIDE == 0 and (first + second) % SIDE == 0)
+
+    def batch(number, visit, skip=None):
         core = (my_core + number // SIDE) % 2
         bys = [ys_by[i] + (my_z + sign * (number + i)) % SIDE for i in range(SIDE)]
         for second in range(SIDE):
             for first in range(SIDE):
                 if isinstance(number, int) and number == first == second == 0:
                     continue
+                if skip is not None and skip(number, first, second):
+                    continue
                 i = (first + second) % SIDE
                 visit(xs[first] + ys_bx[i] + core, bys[i])
 
@@ -132,9 +148,6 @@
 
     def rows_of(chunk, box):
         return pl.ds(pl.multiple_of((chunk * boxes + box) * share, share), share)
-
-    def greet(number, bx, by):
-        pl.semaphore_signal(barrier, inc=1, device_id=(bx, by), device_id_type=MESH)
 
     def scatter(chunk, number, bx, by):
         pltpu.make_async_remote_copy(
@@ -160,11 +173,13 @@
         sent = state.at[chunk, pl.ds(0, count)]
         pltpu.make_async_copy(sent, sent, in_send.at[chunk, number]).wait()
 
-    barrier = pltpu.get_barrier_semaphore()
-    batches(0, BATCHES, greet)
-    pl.semaphore_wait(barrier, boxes - 1)
-
-    batches(0, BATCHES, functools.partial(scatter, 0))
+    for i in range(len(plane)):
+        scatter(0, BATCHES, *plane[i])
+        if i % 2 == 1:
+            scatter(0, BATCHES, *line[i // 2])
+    pl.semaphore_wait(heard, len(line))
+    for number in range(BATCHES):
+        batch(number, functools.partial(scatter, 0, number), on_line_or_plane)
     for chunk in range(CHUNKS):
         pltpu.make_async_copy(coeffs.at[:, rows_of(chunk, me)], state.at[chunk, me], in_recv.at[chunk]).start()
 
@@ -181,11 +196,15 @@
 
     lax.fori_loop(0, LEVELS, tables, 0)
 
+    counts = [
+        sum(not on_line_or_plane(number, i, j) for i in range(SIDE) for j in range(SIDE)) for number in range(BATCHES)
+    ]
+    wait_sent(0, BATCHES, len(plane) + len(line))
     for number in range(EARLY):
-        wait_sent(0, number, BATCH - (number == 0))
+        wait_sent(0, number, counts[number])
     batches(0, BATCHES // 2, functools.partial(scatter, 1))
     for number in range(EARLY, BATCHES):
-        wait_sent(0, number, BATCH)
+        wait_sent(0, number, counts[number])
     batches(BATCHES // 2, BATCHES, functools.partial(scatter, 1))
 
     def work(chunk, carry):
@@ -230,11 +249,12 @@
             pltpu.VMEM((1, width), jnp.int32),
             table,
             table,
-            dma((CHUNKS, BATCHES)),
+            dma((CHUNKS, BATCHES + 1)),
             dma((CHUNKS,)),
             dma((CHUNKS,)),
             dma((CHUNKS,)),
             dma((3,)),
+            pltpu.SemaphoreType.REGULAR,
         ],
         compiler_params=pltpu.CompilerParams(
             collective_id=0, has_side_effects=True, vmem_limit_bytes=48 * 1024 * 1024

time: 106 us -> 105 us (level)
    pallas_call x1, Pallas kernels: 104 us -> 103 us  [local(): pl.pallas_call(functools.partial(kernel, n_bx, n_by), out_shape=jax.Shape...]
where the time goes in v5:
time: 105 us
  Pallas kernels  103 us (98%)
  local copies, waits for them, and re-layouts  2.02 us (2%)
    pallas_call x1, Pallas kernels, local(): pl.pallas_call(functools.partial(kernel, n_bx, n_by), out_shape=jax.Shape...  103 us

profile of v5, /device:TPU:1, one launch (start us, length us, event | category | flops | bytes accessed | tf_op | source)
XLA Modules:
  0.0 104.6 jit_solution(271255563249758619)
XLA Ops:
  0.0 102.6 %butterfly.1 = bf16[2,4096,256]{2,1,0:T(8,128)(2,1)S(1)} custom-call(bf16[2,4096,256]{2,1,0:T(8,128)(2,1)} %bitcast.7, bf16[8,2,2,256,256]{4,3,2,1,0:T(8,128)(2,1)} %interp_hbm.1, s32[8,8,16]{2,1,0:T(8,128)} %bitcast.8, s32[1,256]{1,0:T(1,128)} %bitcast.9), custom_call_target="tpu_custom_call" | custom-call | flops 17179869184 | bytes 16777216 | tf_op jit(solution)/shard_map/butterfly/pallas_call | solution.py:239
  102.6 2.0 %copy.7 = bf16[2,4096,1,1,256]{4,1,3,2,0:T(8,128)(2,1)} copy(bf16[2,4096,1,1,256]{4,1,3,2,0:T(8,128)(2,1)S(1)} %bitcast.6) | data formatting | bytes 8388608

commit v6 on v1

--- a/solution.py
+++ b/solution.py
@@ -16,7 +16,7 @@
 SIDE = 4
 BATCH = SIDE * SIDE
 BATCHES = 2 * SIDE
-EARLY = 6
+EARLY = 4
 MESH = pl.DeviceIdType.MESH
 
 
@@ -81,9 +81,33 @@
     lax.fori_loop(0, boxes // 2 // GROUP, body, 0)
 
 
+def offsets_by_distance():
+    hops = (0, 1, 2, 1)
+    rings = [[] for _ in range(7)]
+    load = [0] * 6
+    steps = range(SIDE)
+    everyone = [(dx, dy, dz, core) for core in range(2) for dz in steps for dy in steps for dx in steps]
+
+    def added(offset):
+        total = list(load)
+        for axis in range(3):
+            total[2 * axis] += offset[axis] in (1, 2)
+            total[2 * axis + 1] += offset[axis] in (2, 3)
+        return total
+
+    for ring in range(7):
+        left = [o for o in everyone if hops[o[0]] + hops[o[1]] + hops[o[2]] + o[3] == ring + 1]
+        while left:
+            best = min(left, key=lambda o: sum(t * t for t in added(o)) - 2 * sum(load) * sum(added(o)) / 6)
+            left.remove(best)
+            load = added(best)
+            rings[ring].append(best)
+    return rings
+
+
 def kernel(
     n_bx, n_by, coeffs, interp_hbm, tgt_hbm, src_hbm, out,
-    state, spare, interp, tgt, src, cosine, sine, in_send, in_recv, out_send, out_recv, load_sem,
+    state, spare, interp, tgt, src, cosine, sine, in_send, in_recv, out_send, out_recv, load_sem, heard,
 ):
     boxes = n_bx * n_by
     share = state.shape[3]
@@ -100,14 +124,16 @@
         pltpu.make_async_copy(tgt_hbm, tgt, load_sem.at[1]),
         pltpu.make_async_copy(interp_hbm, interp, load_sem.at[2]),
     ]
-    for load in loads:
-        load.start()
-
     sign = 1 + (SIDE - 2) * my_core
     xs = [(my_x + sign * i) % SIDE * 4 for i in range(SIDE)]
     ys = [(my_y + sign * i) % SIDE for i in range(SIDE)]
     ys_bx = [y % 2 * 2 for y in ys]
     ys_by = [y // 2 * 4 for y in ys]
+
+    zs = [(my_z + sign * i) % SIDE for i in range(SIDE)]
+    def peer(offset):
+        dx, dy, dz, core = offset
+        return xs[dx] + ys_bx[dy] + (my_core + core) % 2, ys_by[dy] + zs[dz]
 
     def batch(number, visit):
         core = (my_core + number // SIDE) % 2
@@ -133,9 +159,6 @@
     def rows_of(chunk, box):
         return pl.ds(pl.multiple_of((chunk * boxes + box) * share, share), share)
 
-    def greet(number, bx, by):
-        pl.semaphore_signal(barrier, inc=1, device_id=(bx, by), device_id_type=MESH)
-
     def scatter(chunk, number, bx, by):
         pltpu.make_async_remote_copy(
             src_ref=coeffs.at[:, rows_of(chunk, bx * n_by + by)],
@@ -160,11 +183,20 @@
         sent = state.at[chunk, pl.ds(0, count)]
         pltpu.make_async_copy(sent, sent, in_send.at[chunk, number]).wait()
 
+    rings = offsets_by_distance()
+    near = [peer(offset) for offset in rings[0]]
     barrier = pltpu.get_barrier_semaphore()
-    batches(0, BATCHES, greet)
-    pl.semaphore_wait(barrier, boxes - 1)
-
-    batches(0, BATCHES, functools.partial(scatter, 0))
+    for device in near:
+        pl.semaphore_signal(barrier, inc=1, device_id=device, device_id_type=MESH)
+    for load in loads:
+        load.start()
+    for ring, offsets in enumerate(rings):
+        pl.semaphore_wait(barrier if ring == 0 else heard.at[ring], len(near))
+        if ring < len(rings) - 1:
+            for device in near:
+                pl.semaphore_signal(heard.at[ring + 1], inc=1, device_id=device, device_id_type=MESH)
+        for offset in offsets:
+            scatter(0, ring, *peer(offset))
     for chunk in range(CHUNKS):
         pltpu.make_async_copy(coeffs.at[:, rows_of(chunk, me)], state.at[chunk, me], in_recv.at[chunk]).start()
 
@@ -181,11 +213,11 @@
 
     lax.fori_loop(0, LEVELS, tables, 0)
 
-    for number in range(EARLY):
-        wait_sent(0, number, BATCH - (number == 0))
+    for ring in range(EARLY):
+        wait_sent(0, ring, len(rings[ring]))
     batches(0, BATCHES // 2, functools.partial(scatter, 1))
-    for number in range(EARLY, BATCHES):
-        wait_sent(0, number, BATCH)
+    for ring in range(EARLY, len(rings)):
+        wait_sent(0, ring, len(rings[ring]))
     batches(BATCHES // 2, BATCHES, functools.partial(scatter, 1))
 
     def work(chunk, carry):
@@ -235,6 +267,7 @@
             dma((CHUNKS,)),
             dma((CHUNKS,)),
             dma((3,)),
+            pltpu.SemaphoreType.REGULAR((7,)),
         ],
         compiler_params=pltpu.CompilerParams(
             collective_id=0, has_side_effects=True, vmem_limit_bytes=48 * 1024 * 1024

time: 106 us -> 105 us (level)
    pallas_call x1, Pallas kernels: 104 us -> 103 us  [local(): pl.pallas_call(functools.partial(kernel, n_bx, n_by), out_shape=jax.Shape...]
where the time goes in v6:
time: 105 us
  Pallas kernels  103 us (98%)
  local copies, waits for them, and re-layouts  2.02 us (2%)
    pallas_call x1, Pallas kernels, local(): pl.pallas_call(functools.partial(kernel, n_bx, n_by), out_shape=jax.Shape...  103 us

profile of v6, /device:TPU:1, one launch (start us, length us, event | category | flops | bytes accessed | tf_op | source)
XLA Modules:
  0.0 104.6 jit_solution(1995174153790275200)
XLA Ops:
  0.0 102.6 %butterfly.1 = bf16[2,4096,256]{2,1,0:T(8,128)(2,1)S(1)} custom-call(bf16[2,4096,256]{2,1,0:T(8,128)(2,1)} %bitcast.7, bf16[8,2,2,256,256]{4,3,2,1,0:T(8,128)(2,1)} %interp_hbm.1, s32[8,8,16]{2,1,0:T(8,128)} %bitcast.8, s32[1,256]{1,0:T(1,128)} %bitcast.9), custom_call_target="tpu_custom_call" | custom-call | flops 17179869184 | bytes 16777216 | tf_op jit(solution)/shard_map/butterfly/pallas_call | solution.py:252
  102.6 2.0 %copy.7 = bf16[2,4096,1,1,256]{4,1,3,2,0:T(8,128)(2,1)} copy(bf16[2,4096,1,1,256]{4,1,3,2,0:T(8,128)(2,1)S(1)} %bitcast.6) | data formatting | bytes 8388608
